TPU v7x, 256 devices: a whole 4x4x8 slice. The times are simulated.
256 devices in a mesh: section: 4 (over x), fsdp: 64 (over y, z, core).
Axes of the slice: x: 4, y: 4, z: 8, core: 2. Of those that a mesh axis runs over, the one named last changes fastest.
Arguments:
- enc_states: bfloat16 [64, 4, 1280], P('fsdp'), may hold values from -6 to 6
- clip_frames: int32 [64], replicated, may hold values from 2 to 4, as said below
- clip_offset: int32 [64], replicated, may hold values from 0 to 126, as said below
- ln_gain: float32 [1280], replicated, may hold values from 0.1 to 1.9
- ln_bias: float32 [1280], replicated, may hold values from -0.6 to 0.6
- w_proj: bfloat16 [1280, 8192], P(None, 'fsdp'), may hold values from -0.15625 to 0.15625
- proj_bias: float32 [8192], P('fsdp'), may hold values from -3 to 3
- text_embed: bfloat16 [64, 2, 8192], P(None, None, 'fsdp'), may hold values from -6 to 6
- norm_gain: float32 [4, 8192], P('section'), may hold values from 0.1 to 1.9
- w_gate: bfloat16 [4, 14784, 8192], P('section', 'fsdp'), may hold values from -0.0625 to 0.0625
- w_up: bfloat16 [4, 14784, 8192], P('section', 'fsdp'), may hold values from -0.0625 to 0.0625
- w_down: bfloat16 [4, 14784, 8192], P('section', 'fsdp'), may hold values from -0.046875 to 0.046875
Outputs:
- stream_out: bfloat16 [64, 2, 8192], P('section', None, 'fsdp')
Inputs may be any that keep to these rules, and one draw needn't show every extreme that they name: `clip_frames`: every clip's frame count is even, and some clip has exactly 4 frames. Clip c's live rows occupy stream positions clip_offset[c] to clip_offset[c] + clip_frames[c] / 2 - 1, all inside one microbatch (positions m * 64 to (m + 1) * 64 - 1); no two clips share a position; each microbatch holds 32 clips.
All inputs are finite; a program needn't handle non-finite values.
Results may differ from a plain program's by a relative error of at most 0.015.
Values may be sent and summed in bfloat16 or wider, within the bound.
A program may use at most 64 MiB of HBM per device.

v0:
```python
import jax
import jax.numpy as jnp
from jax import lax
from jax.sharding import PartitionSpec as P


def from_behind(value, axis, steps):
    count = lax.axis_size(axis)
    initial, last = (max(0, -steps), min(count, count - steps))
    return lax.ppermute(value, axis, [(source, source + steps) for source in range(initial, last)])


def from_root(value, axis, source):
    kept = jnp.where(lax.axis_index(axis) == source, value, 0).astype(value.dtype)
    return lax.psum(kept, axis)


def rms_scaled(stream, gain):
    values = stream.astype(jnp.float32)
    scale = lax.rsqrt(jnp.mean(values * values, axis=-1, keepdims=True) + 1e-06)
    return (values * scale * gain).astype(jnp.bfloat16)


def on_device(
    enc_states,
    clip_frames,
    clip_offset,
    ln_gain,
    ln_bias,
    w_proj,
    proj_bias,
    text_embed,
    norm_gain,
    w_gate,
    w_up,
    w_down,
):
    section_count = lax.axis_size("section")
    section_index = lax.axis_index("section")
    local_clips, frame_len, enc_width = enc_states.shape
    clip_rows = frame_len // 2
    tokens, micro, feat_local = text_embed.shape
    slots = tokens * micro
    pairs = enc_states.astype(jnp.float32).reshape(local_clips, clip_rows, 2, enc_width)
    pooled = 0.5 * (pairs[:, :, 0] + pairs[:, :, 1])
    centre = jnp.mean(pooled, axis=-1, keepdims=True)
    centred = pooled - centre
    spread = jnp.mean(centred * centred, axis=-1, keepdims=True)
    audio_ln = (centred * lax.rsqrt(spread + 1e-05) * ln_gain + ln_bias).astype(jnp.bfloat16)
    audio_ln = audio_ln.reshape(local_clips * clip_rows, enc_width)
    summed = jnp.dot(
        lax.all_gather(audio_ln, "fsdp", axis=0, tiled=True),
        w_proj,
        preferred_element_type=jnp.float32,
    )
    projected = (summed + proj_bias).astype(jnp.bfloat16)
    within = jnp.arange(clip_rows, dtype=jnp.int32)
    live = within[None, :] * 2 < clip_frames[:, None]
    spot = clip_offset[:, None] + within[None, :]
    target = jnp.where(live, spot % tokens * micro + spot // tokens, slots).reshape(-1)
    flags = jnp.zeros((slots,), jnp.int32).at[target].set(1, mode="drop").reshape(tokens, micro)
    placed = jnp.zeros((slots, feat_local), jnp.bfloat16).at[target].set(projected, mode="drop")
    placed = placed.reshape(tokens, micro, feat_local)
    embedded = jnp.where(flags[:, :, None] == 1, placed, text_embed)
    gain = norm_gain[0]
    gate_w = w_gate[0]
    up_w = w_up[0]
    down_w = w_down[0]
    width = gate_w.shape[1]
    dims = (((1,), (1,)), ((), ()))
    waves = micro // micro
    turns = waves + section_count - 1
    zero_rows = jnp.zeros((tokens, micro, feat_local), jnp.bfloat16)
    incoming = zero_rows
    finished = jnp.zeros((tokens, micro, feat_local), jnp.bfloat16)
    first_section = section_index == 0
    for turn in range(turns):
        if turn < waves:
            fresh = embedded
        else:
            fresh = zero_rows
        current = jnp.where(first_section, fresh, incoming)
        whole = lax.all_gather(current, "fsdp", axis=2, tiled=True)
        layer_normed = rms_scaled(whole, gain).reshape(-1, width)
        gate = lax.dot_general(layer_normed, gate_w, dims, preferred_element_type=jnp.float32)
        up = lax.dot_general(layer_normed, up_w, dims, preferred_element_type=jnp.float32)
        hidden = (jax.nn.silu(gate) * up).astype(jnp.bfloat16)
        partial_sum = jnp.dot(hidden, down_w, preferred_element_type=jnp.float32).reshape(
            tokens, micro, width
        )
        branch = lax.psum_scatter(partial_sum, "fsdp", scatter_dimension=2, tiled=True)
        output = (current.astype(jnp.float32) + branch).astype(jnp.bfloat16)
        leaving = turn - (section_count - 1)
        if leaving >= 0:
            finished = finished.at[:, leaving * micro : (leaving + 1) * micro].set(output)
        if turn + 1 < turns:
            incoming = from_behind(output, "section", 1)
    complete = from_root(finished, "section", section_count - 1)
    rows_each = tokens // section_count
    return lax.dynamic_slice_in_dim(complete, section_index * rows_each, rows_each, 0)


def solution(mesh):
    placed = (
        P("fsdp", None, None),
        P(),
        P(),
        P(),
        P(),
        P(None, "fsdp"),
        P("fsdp"),
        P(None, None, "fsdp"),
        P("section", None),
        P("section", "fsdp", None),
        P("section", "fsdp", None),
        P("section", "fsdp", None),
    )
    return jax.shard_map(
        on_device, mesh=mesh, in_specs=placed, out_specs=P("section", None, "fsdp"), check_vma=False
    )
```

profile of v0, /device:TPU:8, one launch (start us, length us, event | category | flops | bytes accessed | tf_op | source)
XLA Modules:
  0.0 1049.0 jit_solution(15921234189649798289)
XLA Ops:
  8.4 50.3 %all-gather = bf16[64,2,1280]{2,1,0:T(2,128)(2,1)S(1)} all-gather(bf16[1,2,1280]{2,1,0:T(2,128)(2,1)S(1)} %fusion.76), channel_id=1, replica_groups=mesh['section'=4,'fsdp'=64] {'fsdp'}, dimensions={0}, use_global_device_ids=true | all-gather | bytes 332800 | tf_op jit(solution)/shard_map/all_gather | solution.py:52
  60.6 1.0 scatter_custom_fusion
  61.9 0.9 fusion.60
  62.8 0.9 scatter_custom_fusion.1
  63.7 1.4 fusion.66
  65.2 71.5 %all-gather.6.cloned.1.call-done = bf16[64,2,8192]{2,0,1:T(8,128)(2,1)} async-done(((bf16[64,2,128]{2,0,1:T(8,128)(2,1)}), bf16[64,2,8192]{2,0,1:T(8,128)(2,1)}) %all-gather.6.cloned.1.call-update) | async-done | bytes 2097168 | tf_op jit(solution)/shard_map/all_gather | solution.py:83
  136.7 2.1 fusion
  138.8 2.2 fusion.2
  141.0 3.5 copy.55
  144.5 2.7 reshape.369
  147.3 3.5 fusion.34
  150.7 1.3 fusion.57
  152.2 4.8 fusion.18
  157.1 141.9 %reduce-scatter.5.cloned.1.call-done = f32[64,2,128]{2,0,1:T(8,128)} async-done(((f32[64,2,8192]{2,0,1:T(8,128)}), f32[64,2,128]{2,0,1:T(8,128)}) %reduce-scatter.5.cloned.1.call-update) | async-done | bytes 65552 | tf_op jit(solution)/shard_map/reduce_scatter | solution.py:91
  299.9 3.4 collective-permute-start
  303.3 1.6 collective-permute-done
  305.7 72.4 %all-gather.8.cloned.1.call-done = bf16[64,2,8192]{2,0,1:T(8,128)(2,1)} async-done(((bf16[64,2,128]{2,0,1:T(8,128)(2,1)}), bf16[64,2,8192]{2,0,1:T(8,128)(2,1)}) %all-gather.8.cloned.1.call-update) | async-done | bytes 2097168 | tf_op jit(solution)/shard_map/all_gather | solution.py:83
  378.2 2.1 fusion.3
  380.3 2.2 fusion.5
  382.4 3.5 copy.58
  386.0 2.7 reshape.370
  388.7 3.5 fusion.32
  392.2 1.3 fusion.54
  393.7 4.8 fusion.16
  398.6 142.0 %reduce-scatter.7.cloned.1.call-done = f32[64,2,128]{2,0,1:T(8,128)} async-done(((f32[64,2,8192]{2,0,1:T(8,128)}), f32[64,2,128]{2,0,1:T(8,128)}) %reduce-scatter.7.cloned.1.call-update) | async-done | bytes 65552 | tf_op jit(solution)/shard_map/reduce_scatter | solution.py:91
  541.5 3.3 collective-permute-start.1
  544.8 1.6 collective-permute-done.1
  547.3 72.4 %all-gather.10.cloned.1.call-done = bf16[64,2,8192]{2,0,1:T(8,128)(2,1)} async-done(((bf16[64,2,128]{2,0,1:T(8,128)(2,1)}), bf16[64,2,8192]{2,0,1:T(8,128)(2,1)}) %all-gather.10.cloned.1.call-update) | async-done | bytes 2097168 | tf_op jit(solution)/shard_map/all_gather | solution.py:83
  619.7 2.1 fusion.6
  621.9 2.2 fusion.8
  624.0 3.5 copy.61
  627.6 2.7 reshape.371
  630.3 3.4 fusion.30
  633.8 1.3 fusion.51
  635.3 4.8 fusion.14
  640.2 142.1 %reduce-scatter.9.cloned.1.call-done = f32[64,2,128]{2,0,1:T(8,128)} async-done(((f32[64,2,8192]{2,0,1:T(8,128)}), f32[64,2,128]{2,0,1:T(8,128)}) %reduce-scatter.9.cloned.1.call-update) | async-done | bytes 65552 | tf_op jit(solution)/shard_map/reduce_scatter | solution.py:91
  783.1 3.3 collective-permute-start.2
  786.4 1.6 collective-permute-done.2
  788.9 72.3 %all-gather.12.cloned.1.call-done = bf16[64,2,8192]{2,0,1:T(8,128)(2,1)} async-done(((bf16[64,2,128]{2,0,1:T(8,128)(2,1)}), bf16[64,2,8192]{2,0,1:T(8,128)(2,1)}) %all-gather.12.cloned.1.call-update) | async-done | bytes 2097168 | tf_op jit(solution)/shard_map/all_gather | solution.py:83
  861.2 2.1 fusion.9
  863.4 2.2 fusion.11
  865.5 3.5 copy.64
  869.1 2.7 reshape.372
  871.8 3.5 fusion.28
  875.3 1.3 fusion.48
  876.8 4.8 fusion.12
  881.6 142.0 %reduce-scatter.11.cloned.1.call-done = f32[64,2,128]{2,0,1:T(8,128)} async-done(((f32[64,2,8192]{2,0,1:T(8,128)}), f32[64,2,128]{2,0,1:T(8,128)}) %reduce-scatter.11.cloned.1.call-update) | async-done | bytes 65552 | tf_op jit(solution)/shard_map/reduce_scatter | solution.py:91
  1024.5 17.0 %psum.7 = bf16[64,2,128]{2,0,1:T(8,128)(2,1)S(1)} all-reduce(bf16[64,2,128]{2,0,1:T(8,128)(2,1)S(1)} %fusion.65), channel_id=1, replica_groups=mesh['section'=4,'fsdp'=64] {'section'}, use_global_device_ids=true, to_apply=%region_12.13 | all-reduce | flops 16384 | bytes 65536 | tf_op jit(solution)/shard_map/psum | solution.py:15
  (68 shorter events, 11.6 us)
Async XLA Ops:
  6.5 55.3 %copy-start = (bf16[1280,128]{1,0:T(8,128)(2,1)S(1)}, bf16[1280,128]{1,0:T(8,128)(2,1)}, u32[]{:S(2)}) copy-start(bf16[1280,128]{1,0:T(8,128)(2,1)} %param.21) | copy-start | bytes 983044
  6.5 132.3 %copy-start.5 = (f32[1,8192]{1,0:T(1,128)S(1)}, f32[1,8192]{1,0:T(1,128)}, u32[]{:S(2)}) copy-start(f32[1,8192]{1,0:T(1,128)} %param.24) | copy-start | bytes 98308
  6.5 130.1 %all-gather.6.cloned.1.call-start = ((), (), s32[]{:S(2)}) async-start(), calls=%async_computation.4 | async-start | bytes 2129920 | tf_op jit(solution)/shard_map/all_gather | solution.py:83
  65.2 233.9 %reduce-scatter.5.cloned.1.call-start = ((), (), s32[]{:S(2)}) async-start(), calls=%async_computation.5 | async-start | bytes 4259840 | tf_op jit(solution)/shard_map/reduce_scatter | solution.py:91
  147.3 3.5 copy-start.1
  157.0 142.0 %copy-start.6 = (bf16[64,2,128]{2,0,1:T(8,128)(2,1)S(1)}, bf16[64,2,128]{2,0,1:T(8,128)(2,1)}, u32[]{:S(2)}) copy-start(bf16[64,2,128]{2,0,1:T(8,128)(2,1)} %fusion.66) | copy-start | bytes 98308
  157.1 221.1 %all-gather.8.cloned.1.call-start = ((), (), s32[]{:S(2)}) async-start(), calls=%async_computation.6 | async-start | bytes 2129920 | tf_op jit(solution)/shard_map/all_gather | solution.py:83
  299.9 5.0 collective-permute-start
  305.5 235.1 %reduce-scatter.7.cloned.1.call-start = ((), (), s32[]{:S(2)}) async-start(), calls=%async_computation.7 | async-start | bytes 4259840 | tf_op jit(solution)/shard_map/reduce_scatter | solution.py:91
  388.7 3.5 copy-start.2
  398.5 221.2 %all-gather.10.cloned.1.call-start = ((), (), s32[]{:S(2)}) async-start(), calls=%async_computation.8 | async-start | bytes 2129920 | tf_op jit(solution)/shard_map/all_gather | solution.py:83
  541.5 4.9 collective-permute-start.1
  547.0 235.2 %reduce-scatter.9.cloned.1.call-start = ((), (), s32[]{:S(2)}) async-start(), calls=%async_computation.9 | async-start | bytes 4259840 | tf_op jit(solution)/shard_map/reduce_scatter | solution.py:91
  630.3 3.5 copy-start.3
  640.1 221.1 %all-gather.12.cloned.1.call-start = ((), (), s32[]{:S(2)}) async-start(), calls=%async_computation.10 | async-start | bytes 2129920 | tf_op jit(solution)/shard_map/all_gather | solution.py:83
  783.1 4.9 collective-permute-start.2
  788.6 235.0 %reduce-scatter.11.cloned.1.call-start = ((), (), s32[]{:S(2)}) async-start(), calls=%async_computation.11 | async-start | bytes 4259840 | tf_op jit(solution)/shard_map/reduce_scatter | solution.py:91
  871.8 3.5 copy-start.4
Sparse Core Ops, SparseCore 0:
  65.3 71.3 all-gather.5
  157.2 141.8 reduce-scatter.4
  305.6 72.5 all-gather.7
  398.7 141.9 reduce-scatter.6
  547.1 72.5 all-gather.9
  640.2 141.9 reduce-scatter.8
  788.7 72.4 all-gather.11
  881.7 141.8 reduce-scatter.10
where the time goes:
time: 1050 us
  waiting for transfers between devices  862 us (82%)
  blocking collectives  67.3 us (6%)
  matrix products  39.3 us (4%)
  local copies, waits for them, and re-layouts  29.6 us (3%)
  other arithmetic  26.4 us (3%)
  between operations  13.9 us (1%)
  starting transfers between devices  10.9 us (1%)
    reduce_scatter x4, waiting for transfers between devices, on_device(): lax.psum_scatter(partial_sum, 'fsdp', scatter_dimension=2, tiled=True)  568 us
    all_gather x4, waiting for transfers between devices, on_device(): whole = lax.all_gather(current, 'fsdp', axis=2, tiled=True)  289 us
    all_gather x1, blocking collectives, on_device(): lax.all_gather(audio_ln, 'fsdp', axis=0, tiled=True)  50.3 us
  transfers between devices with their start and end apart: 11, of which 11 were waited for; matrix products, arithmetic and copies ran while one was open for 0% of the time, Pallas kernels for 0%

commit v1 on v0

--- a/solution.py
+++ b/solution.py
@@ -80,7 +80,9 @@
         else:
             fresh = zero_rows
         current = jnp.where(first_section, fresh, incoming)
-        whole = lax.all_gather(current, "fsdp", axis=2, tiled=True)
+        whole = jnp.concatenate(
+            lax.all_to_all(jnp.stack([current] * lax.axis_size("fsdp")), "fsdp", 0, 0), axis=2
+        )
         layer_normed = rms_scaled(whole, gain).reshape(-1, width)
         gate = lax.dot_general(layer_normed, gate_w, dims, preferred_element_type=jnp.float32)
         up = lax.dot_general(layer_normed, up_w, dims, preferred_element_type=jnp.float32)

time: 1050 us -> 991 us (0.944)
  waiting for transfers between devices: 862 us -> 573 us
  blocking collectives: 67.3 us -> 299 us
    all_gather x4 -> x0, waiting for transfers between devices: 289 us -> none  [on_device(): whole = lax.all_gather(current, 'fsdp', axis=2, tiled=True)]
    all_to_all x0 -> x4, blocking collectives: none -> 231 us  [on_device(): lax.all_to_all(jnp.stack([current] * lax.axis_size('fsdp')), 'fsdp', 0, 0)]
    reshape x4 -> x0, local copies, waits for them, and re-layouts: 11 us -> none  [on_device(): layer_normed = rms_scaled(whole, gain).reshape(-1, width)]
  transfers between devices with their start and end apart: 11 -> 7, of which waited for: 11 -> 7; matrix products, arithmetic and copies ran while one was open for 0% -> 0% of each run, Pallas kernels for 0% -> 0%
where the time goes in v1:
time: 991 us; the launch traced here: 986 us
  waiting for transfers between devices  573 us (58%)
  blocking collectives  299 us (30%)
  matrix products  35.3 us (4%)
  other arithmetic  31.6 us (3%)
  local copies, waits for them, and re-layouts  22.8 us (2%)
  between operations  13.8 us (1%)
  starting transfers between devices  10.3 us (1%)
    reduce_scatter x4, waiting for transfers between devices, on_device(): lax.psum_scatter(partial_sum, 'fsdp', scatter_dimension=2, tiled=True)  568 us
    all_to_all x4, blocking collectives, on_device(): lax.all_to_all(jnp.stack([current] * lax.axis_size('fsdp')), 'fsdp', 0, 0)  231 us
    all_gather x1, blocking collectives, on_device(): lax.all_gather(audio_ln, 'fsdp', axis=0, tiled=True)  50.3 us
  transfers between devices with their start and end apart: 7, of which 7 were waited for; matrix products, arithmetic and copies ran while one was open for 0% of the time, Pallas kernels for 0%

profile of v1, /device:TPU:8, one launch (start us, length us, event | category | flops | bytes accessed | tf_op | source)
XLA Modules:
  0.0 985.6 jit_solution(11656536664478741694)
XLA Ops:
  8.4 50.3 %all-gather = bf16[64,2,1280]{2,1,0:T(2,128)(2,1)S(1)} all-gather(bf16[1,2,1280]{2,1,0:T(2,128)(2,1)S(1)} %fusion.112), channel_id=1, replica_groups=mesh['section'=4,'fsdp'=64] {'fsdp'}, dimensions={0}, use_global_device_ids=true | all-gather | bytes 332800 | tf_op jit(solution)/shard_map/all_gather | solution.py:52
  60.6 1.0 scatter_custom_fusion
  61.9 0.9 fusion.96
  62.8 0.9 scatter_custom_fusion.1
  64.6 2.0 stack.8
  66.6 57.5 %all_to_all.20 = bf16[64,64,2,128]{3,2,1,0:T(2,128)(2,1)S(1)} all-to-all(bf16[64,64,2,128]{3,2,1,0:T(2,128)(2,1)S(1)} %stack.8), channel_id=1, replica_groups=mesh['section'=4,'fsdp'=64] {'fsdp'}, dimensions={0} | all-to-all | bytes 4194304 | tf_op jit(solution)/shard_map/all_to_all | solution.py:84
  124.2 2.3 fusion
  126.5 3.9 fusion.39
  130.4 2.4 copy.110
  132.8 2.0 fusion.34
  134.9 1.8 fusion.91
  136.9 4.8 fusion.18
  141.8 141.4 %reduce-scatter.5.cloned.1.call-done = f32[64,2,128]{2,0,1:T(8,128)} async-done(((f32[64,2,8192]{2,0,1:T(8,128)}), f32[64,2,128]{2,0,1:T(8,128)}) %reduce-scatter.5.cloned.1.call-update) | async-done | bytes 65552 | tf_op jit(solution)/shard_map/reduce_scatter | solution.py:93
  284.0 3.4 collective-permute-start
  287.4 1.6 collective-permute-done
  289.1 2.0 stack.9
  291.1 58.1 %all_to_all.21 = bf16[64,64,2,128]{3,2,1,0:T(2,128)(2,1)S(1)} all-to-all(bf16[64,64,2,128]{3,2,1,0:T(2,128)(2,1)S(1)} %stack.9), channel_id=1, replica_groups=mesh['section'=4,'fsdp'=64] {'fsdp'}, dimensions={0} | all-to-all | bytes 4194304 | tf_op jit(solution)/shard_map/all_to_all | solution.py:84
  349.2 2.3 fusion.3
  351.5 3.9 fusion.38
  355.4 2.4 copy.116
  357.9 2.0 fusion.32
  359.9 1.8 fusion.86
  361.9 4.8 fusion.16
  366.8 142.3 %reduce-scatter.7.cloned.1.call-done = f32[64,2,128]{2,0,1:T(8,128)} async-done(((f32[64,2,8192]{2,0,1:T(8,128)}), f32[64,2,128]{2,0,1:T(8,128)}) %reduce-scatter.7.cloned.1.call-update) | async-done | bytes 65552 | tf_op jit(solution)/shard_map/reduce_scatter | solution.py:93
  509.9 3.4 collective-permute-start.1
  513.4 1.6 collective-permute-done.1
  515.0 2.0 stack.10
  517.0 57.9 %all_to_all.22 = bf16[64,64,2,128]{3,2,1,0:T(2,128)(2,1)S(1)} all-to-all(bf16[64,64,2,128]{3,2,1,0:T(2,128)(2,1)S(1)} %stack.10), channel_id=1, replica_groups=mesh['section'=4,'fsdp'=64] {'fsdp'}, dimensions={0} | all-to-all | bytes 4194304 | tf_op jit(solution)/shard_map/all_to_all | solution.py:84
  574.9 2.3 fusion.6
  577.2 3.9 fusion.37
  581.1 2.4 copy.122
  583.6 2.0 fusion.30
  585.6 1.8 fusion.81
  587.6 4.8 fusion.14
  592.5 142.2 %reduce-scatter.9.cloned.1.call-done = f32[64,2,128]{2,0,1:T(8,128)} async-done(((f32[64,2,8192]{2,0,1:T(8,128)}), f32[64,2,128]{2,0,1:T(8,128)}) %reduce-scatter.9.cloned.1.call-update) | async-done | bytes 65552 | tf_op jit(solution)/shard_map/reduce_scatter | solution.py:93
  735.6 3.4 collective-permute-start.2
  738.9 1.6 collective-permute-done.2
  740.6 2.0 stack.11
  742.6 57.9 %all_to_all.23 = bf16[64,64,2,128]{3,2,1,0:T(2,128)(2,1)S(1)} all-to-all(bf16[64,64,2,128]{3,2,1,0:T(2,128)(2,1)S(1)} %stack.11), channel_id=1, replica_groups=mesh['section'=4,'fsdp'=64] {'fsdp'}, dimensions={0} | all-to-all | bytes 4194304 | tf_op jit(solution)/shard_map/all_to_all | solution.py:84
  800.5 2.3 fusion.9
  802.8 3.9 fusion.36
  806.7 2.4 copy.128
  809.2 2.0 fusion.28
  811.3 1.8 fusion.76
  813.2 4.8 fusion.12
  818.1 142.3 %reduce-scatter.11.cloned.1.call-done = f32[64,2,128]{2,0,1:T(8,128)} async-done(((f32[64,2,8192]{2,0,1:T(8,128)}), f32[64,2,128]{2,0,1:T(8,128)}) %reduce-scatter.11.cloned.1.call-update) | async-done | bytes 65552 | tf_op jit(solution)/shard_map/reduce_scatter | solution.py:93
  960.4 0.9 fusion.101
  961.2 17.0 %psum.7 = bf16[64,2,128]{2,0,1:T(8,128)(2,1)S(1)} all-reduce(bf16[64,2,128]{2,0,1:T(8,128)(2,1)S(1)} %fusion.101), channel_id=1, replica_groups=mesh['section'=4,'fsdp'=64] {'section'}, use_global_device_ids=true, to_apply=%region_12.13 | all-reduce | flops 16384 | bytes 65536 | tf_op jit(solution)/shard_map/psum | solution.py:15
  (70 shorter events, 9.4 us)
Async XLA Ops:
  6.5 55.3 %copy-start = (bf16[1280,128]{1,0:T(8,128)(2,1)S(1)}, bf16[1280,128]{1,0:T(8,128)(2,1)}, u32[]{:S(2)}) copy-start(bf16[1280,128]{1,0:T(8,128)(2,1)} %param.21) | copy-start | bytes 983044
  6.5 276.7 %reduce-scatter.5.cloned.1.call-start = ((), (), s32[]{:S(2)}) async-start(), calls=%async_computation.8 | async-start | bytes 4259840 | tf_op jit(solution)/shard_map/reduce_scatter | solution.py:93
  64.6 61.9 %copy-start.1 = (f32[1,8192]{1,0:T(1,128)S(1)}, f32[1,8192]{1,0:T(1,128)}, u32[]{:S(2)}) copy-start(f32[1,8192]{1,0:T(1,128)} %param.24) | copy-start | bytes 98308
  126.4 6.4 copy-start.2
  132.8 2.1 copy-start.6
  141.7 367.4 %reduce-scatter.7.cloned.1.call-start = ((), (), s32[]{:S(2)}) async-start(), calls=%async_computation.9 | async-start | bytes 4259840 | tf_op jit(solution)/shard_map/reduce_scatter | solution.py:93
  284.0 5.0 collective-permute-start
  351.5 6.4 copy-start.3
  357.9 2.1 copy-start.7
  366.8 367.9 %reduce-scatter.9.cloned.1.call-start = ((), (), s32[]{:S(2)}) async-start(), calls=%async_computation.10 | async-start | bytes 4259840 | tf_op jit(solution)/shard_map/reduce_scatter | solution.py:93
  509.9 5.0 collective-permute-start.1
  577.2 6.4 copy-start.4
  583.5 2.1 copy-start.8
  592.4 367.9 %reduce-scatter.11.cloned.1.call-start = ((), (), s32[]{:S(2)}) async-start(), calls=%async_computation.11 | async-start | bytes 4259840 | tf_op jit(solution)/shard_map/reduce_scatter | solution.py:93
  735.6 5.0 collective-permute-start.2
  802.8 6.4 copy-start.5
  809.2 2.1 copy-start.9
Sparse Core Ops, SparseCore 0:
  141.8 141.3 reduce-scatter.4
  366.9 142.1 reduce-scatter.6
  592.6 142.0 reduce-scatter.8
  818.2 142.1 reduce-scatter.10
